TPU v7x, 512 devices: a whole 4x4x16 slice. The times are simulated.
512 devices in a mesh: date: 128 (over z, y, x_lo), az: 4 (over x_hi, core).
Axes of the slice: x: 4 (x_hi: 2, x_lo: 2; x = x_hi * 2 + x_lo), y: 4, z: 16, core: 2. Of those that a mesh axis runs over, the one named last changes fastest.
Arguments:
- slabs: float32 [128, 2, 128, 2048], P('date', None, 'az'), may hold values from -6 to 6
Outputs:
- interferos: float32 [5, 2, 128, 32, 128], P(None, None, 'date', 'az')
- coherence: float32 [5, 128, 32, 128], P(None, 'date', 'az')
All inputs are finite; a program needn't handle non-finite values.
Results may differ from a plain program's by a relative error of at most 0.0003.
Values sent between devices are 32-bit elements; how exact they have to be, the bound alone decides.
No kernel may reach another device: no remote copies, remote signals or barrier semaphores. Data moves between devices by JAX's collectives and lax.ppermute only.
A program may use at most 64 MiB of HBM per device.

v0:
```python
import functools

import jax
import jax.numpy as jnp
from jax import lax
from jax.experimental import pallas as pl
from jax.experimental.pallas import tpu as pltpu
from jax.sharding import PartitionSpec as P

LOOK_AZ = 4
LOOK_RG = 16
WIN = 5
SPAN = 5
GROUP = 8
FIELDS = 3 * SPAN + 1
SUB = 16


def cut_kernel(slab_ref, out_ref, held, arrived):
    planes, lines, _ = slab_ref.shape
    width = out_ref.shape[-1]
    blocks = SUB // 2
    parts = [(p, line, b) for line in range(0, lines, 8) for p in range(planes) for b in range(0, SUB, blocks)]
    copies = []
    for plane, line, first in parts:
        here = (plane, pl.ds(line, 8), pl.ds(first * width, blocks * width))
        copies.append(pltpu.make_async_copy(slab_ref.at[here], held.at[here], arrived.at[len(copies)]))
        copies[-1].start(priority=first // blocks)
    for (plane, line, first), copy in zip(parts, copies):
        copy.wait()
        for block in range(first, first + blocks):
            part = held[plane, line : line + 8, block * width : (block + 1) * width]
            start = (line * planes + plane) * SUB + block
            out_ref[pl.ds(start, 8, stride=planes * SUB), :] = part


def cut(slab):
    planes, lines, samples = slab.shape
    rows = planes * lines * SUB
    slab = pltpu.with_memory_space_constraint(slab, pltpu.HBM)
    return pl.pallas_call(
        cut_kernel,
        in_specs=[pl.BlockSpec(memory_space=pl.ANY)],
        out_shape=jax.ShapeDtypeStruct((rows, samples // SUB), jnp.float32),
        scratch_shapes=[
            pltpu.VMEM(slab.shape, jnp.float32),
            pltpu.SemaphoreType.DMA((planes * lines // 4,)),
        ],
        compiler_params=pltpu.CompilerParams(vmem_limit_bytes=4 * 1024 * 1024),
        name="cut",
    )(slab)


def inside(index):
    return min(SPAN, GROUP - 1 - index)


def look_at(date, pairs, powers, sums, cols):
    width = sums.shape[-1]
    count = 0

    def put(terms):
        nonlocal count
        total = terms[0]
        for term in terms[1:]:
            total = total + term
        sums[count * SUB : (count + 1) * SUB, :] = total
        count += 1

    for index, gaps in pairs:
        real, imag = date(index)
        others = [date(index + gap) for gap in gaps]
        for other_real, other_imag in others:
            put([a * b for a, b in zip(real + imag, other_real + other_imag)])
        for other_real, other_imag in others:
            put([a * b - c * d for a, b, c, d in zip(imag, other_real, real, other_imag)])
    for index in powers:
        real, imag = date(index)
        put([v * v for v in real + imag])

    per_block = width // LOOK_RG
    sample = lax.broadcasted_iota(jnp.int32, (width, cols), 0)
    lane = lax.broadcasted_iota(jnp.int32, (width, cols), 1)
    weight = jnp.where(sample // LOOK_RG == lane % per_block, 1.0 / (LOOK_AZ * LOOK_RG), 0.0)
    weight = weight.astype(jnp.bfloat16)
    total = sums[: count * SUB, :]
    high = total.astype(jnp.bfloat16)
    low = (total - high.astype(jnp.float32)).astype(jnp.bfloat16)
    looks = jnp.dot(high, weight, preferred_element_type=jnp.float32)
    looks = looks + jnp.dot(low, weight, preferred_element_type=jnp.float32)
    looks = looks.reshape(count, SUB, cols)
    block = lax.broadcasted_iota(jnp.int32, (1, SUB, cols), 1)
    lane = lax.broadcasted_iota(jnp.int32, (1, SUB, cols), 2)
    return jnp.sum(jnp.where(lane // per_block == block, looks, 0.0), axis=1)


def planes_of(ref, at):
    return [ref[at, 2 * k] for k in range(LOOK_AZ)], [ref[at, 2 * k + 1] for k in range(LOOK_AZ)]


OWN_PAIRS = [(d, range(1, inside(d) + 1)) for d in range(GROUP)]
LATER_PAIRS = [(d, range(inside(d) + 1, SPAN + 1)) for d in range(GROUP) if inside(d) < SPAN]
OWN_ROWS = sum(2 * len(gaps) for _, gaps in OWN_PAIRS)
LATER_ROWS = sum(2 * len(gaps) for _, gaps in LATER_PAIRS)


def own_kernel(own_ref, out_ref, sums):
    out_ref[...] = look_at(lambda d: planes_of(own_ref, d), OWN_PAIRS, range(GROUP), sums, out_ref.shape[-1])


def later_kernel(own_ref, later_ref, looks_ref, out_ref, sums, cells):
    def date(index):
        return planes_of(own_ref, index) if index < GROUP else planes_of(later_ref, index - GROUP)

    cells[...] = look_at(date, LATER_PAIRS, range(GROUP, GROUP + SPAN), sums, out_ref.shape[-1])
    own_at = later_at = 0
    for index in range(GROUP):
        near, far = inside(index), SPAN - inside(index)
        piece = out_ref.at[index, 0]
        for part in range(2):
            if near:
                piece[part * SPAN : part * SPAN + near, :] = looks_ref[own_at : own_at + near, :]
            if far:
                piece[part * SPAN + near : (part + 1) * SPAN, :] = cells[later_at : later_at + far, :]
            own_at += near
            later_at += far
        piece[2 * SPAN : 2 * SPAN + 1 + near, :] = looks_ref[OWN_ROWS + index : OWN_ROWS + index + 1 + near, :]
        if far:
            piece[2 * SPAN + 1 + near :, :] = cells[LATER_ROWS : LATER_ROWS + far, :]
        for tile in range(1, out_ref.shape[1]):
            out_ref[index, tile] = out_ref[index, 0]


def look_own(own, cols):
    rows = OWN_ROWS + GROUP
    return pl.pallas_call(
        own_kernel,
        out_shape=jax.ShapeDtypeStruct((rows, cols), jnp.float32),
        scratch_shapes=[pltpu.VMEM((rows * SUB, own.shape[-1]), jnp.float32)],
        compiler_params=pltpu.CompilerParams(vmem_limit_bytes=8 * 1024 * 1024),
        cost_estimate=pl.CostEstimate(
            flops=12 * rows * SUB * cols * cols, bytes_accessed=own.size * 4, transcendentals=0
        ),
        name="look_own",
    )(own)


def look_later(own, later, looks, tiles):
    cols = looks.shape[-1]
    rows = LATER_ROWS + SPAN
    return pl.pallas_call(
        later_kernel,
        out_shape=jax.ShapeDtypeStruct((GROUP, tiles, FIELDS, cols), jnp.float32),
        scratch_shapes=[
            pltpu.VMEM((rows * SUB, own.shape[-1]), jnp.float32),
            pltpu.VMEM((rows, cols), jnp.float32),
        ],
        compiler_params=pltpu.CompilerParams(vmem_limit_bytes=8 * 1024 * 1024),
        name="look_later",
    )(own, later, looks)


def coherence_kernel(tiles, rows_ref, looks_out, coher_out, looks_ref, values, coher_ref, sent):
    date, dates = lax.axis_index("date"), lax.axis_size("date")
    tile = lax.axis_index("az")
    cols = rows_ref.shape[-1]
    half = WIN // 2
    for gap in range(1, SPAN + 1):
        for part in range(2):
            start = tile * FIELDS + part * SPAN + gap - 1
            look = rows_ref[pl.ds(start, GROUP, stride=tiles * FIELDS), :]
            looks_ref[gap - 1, part, 0] = jnp.where(date + gap < dates, look, 0.0)
    looks_sent = pltpu.make_async_copy(looks_ref, looks_out, sent.at[0])
    looks_sent.start()

    lane = lax.broadcasted_iota(jnp.int32, (FIELDS, cols), 1)
    rows = []
    for offset in range(-half, GROUP + half):
        other = tile + offset // GROUP
        start = (offset % GROUP * tiles + jnp.clip(other, 0, tiles - 1)) * FIELDS
        row = rows_ref[pl.ds(pl.multiple_of(start, FIELDS), FIELDS), :]
        if not 0 <= offset < GROUP:
            row = jnp.where(jnp.logical_and(other >= 0, other < tiles), row, 0.0)
        rows.append(row)
    for r in range(GROUP):
        tall = rows[r]
        for shift in range(1, WIN):
            tall = tall + rows[r + shift]
        boxed = tall
        for shift in range(1, half + 1):
            boxed = boxed + jnp.where(lane >= shift, pltpu.roll(tall, shift, 1), 0.0)
            boxed = boxed + jnp.where(lane < cols - shift, pltpu.roll(tall, cols - shift, 1), 0.0)
        real = boxed[:SPAN]
        imag = boxed[SPAN : 2 * SPAN]
        own = boxed[2 * SPAN : 2 * SPAN + 1]
        later = boxed[2 * SPAN + 1 :]
        value = jnp.sqrt(real * real + imag * imag) / jnp.sqrt(own * later + 1e-06)
        values[r * GROUP : r * GROUP + SPAN, :] = value
    for gap in range(1, SPAN + 1):
        value = values[pl.ds(gap - 1, GROUP, stride=GROUP), :]
        coher_ref[gap - 1, 0] = jnp.where(date + gap < dates, value, 0.0)
    coher_sent = pltpu.make_async_copy(coher_ref, coher_out, sent.at[1])
    coher_sent.start()
    looks_sent.wait()
    coher_sent.wait()


def finish(rows, tiles):
    cols = rows.shape[-1]
    looks = (SPAN, 2, 1, GROUP, cols)
    coher = (SPAN, 1, GROUP, cols)
    return pl.pallas_call(
        functools.partial(coherence_kernel, tiles),
        out_shape=(jax.ShapeDtypeStruct(looks, jnp.float32), jax.ShapeDtypeStruct(coher, jnp.float32)),
        out_specs=(pl.BlockSpec(memory_space=pl.ANY), pl.BlockSpec(memory_space=pl.ANY)),
        scratch_shapes=[
            pltpu.VMEM(looks, jnp.float32),
            pltpu.VMEM((GROUP * GROUP, cols), jnp.float32),
            pltpu.VMEM(coher, jnp.float32),
            pltpu.SemaphoreType.DMA((2,)),
        ],
        compiler_params=pltpu.CompilerParams(vmem_limit_bytes=4 * 1024 * 1024),
        name="finish",
    )(rows)


def local(slabs):
    dates, tiles = lax.axis_size("date"), lax.axis_size("az")
    _, planes, lines, samples = slabs.shape
    cols = samples // LOOK_RG
    groups = [list(range(g, g + GROUP)) for g in range(0, dates, GROUP)]
    wide = [list(range(g * tiles, (g + GROUP) * tiles)) for g in range(0, dates, GROUP)]
    pieces = cut(slabs[0]).reshape(GROUP, LOOK_AZ * planes, SUB, samples // SUB)
    own = lax.all_to_all(pieces, "date", 0, 0, axis_index_groups=groups, tiled=True)
    back = [(i, i - GROUP) for i in range(GROUP, dates)]
    later = lax.ppermute(own[:SPAN], "date", back)
    fields = look_later(own, later, look_own(own, cols), tiles)
    fields = fields.reshape(GROUP * tiles, FIELDS, cols)
    rows = lax.all_to_all(fields, ("date", "az"), 0, 0, axis_index_groups=wide, tiled=True)
    return finish(rows.reshape(GROUP * tiles * FIELDS, cols), tiles)


def solution(mesh):
    in_specs = (P("date", None, "az", None),)
    out_specs = (P(None, None, "date", "az", None), P(None, "date", "az", None))
    return jax.shard_map(local, mesh=mesh, in_specs=in_specs, out_specs=out_specs, check_vma=False)
```

profile of v0, /device:TPU:1, one launch (start us, length us, event | category | flops | bytes accessed | tf_op | source)
XLA Modules:
  0.0 43.2 jit_solution(10192775024098382915)
XLA Ops:
  0.6 1.3 %cut.1 = f32[1024,128]{1,0:T(8,128)S(1)} custom-call(f32[2,32,2048]{2,1,0:T(8,128)} %bitcast.7), custom_call_target="tpu_custom_call" | custom-call | tf_op jit(solution)/shard_map/cut/pallas_call | solution.py:41
  2.0 13.3 %all_to_all.10.own_ref = f32[8,8,16,128]{3,2,1,0:T(8,128)S(1)} all-to-all(f32[8,8,16,128]{3,2,1,0:T(8,128)S(1)} %bitcast.4), channel_id=1, replica_groups={{0,4,8,12,16,20,24,28},{32,36,40,44,48,52,56,60},{64,68,72,76,80,84,88,..., dimensions={0} | all-to-all | bytes 1048576 | tf_op jit(solution)/shard_map/all_to_all | solution.py:234
  15.3 1.3 %collective-permute-start = (f32[5,8,16,128]{3,2,1,0:T(8,128)S(1)}, f32[5,8,16,128]{3,2,1,0:T(8,128)S(1)}, u32[]{:S(2)}, u32[]{:S(2)}) collective-permute-start(f32[5,8,16,128]{3,2,1,0:T(8,128)S(1)} %slice.4), channel_id=1, source_target_pairs={{32,0},{36,4},{40,8},{44,12},{48,16},{52,20},{56,24},{60,28},{64,3... | collective-permute-start | bytes 983048 | tf_op jit(solution)/shard_map/ppermute | solution.py:236
  16.6 0.4 %look_own.1.looks_ref = f32[58,128]{1,0:T(8,128)S(1)} custom-call(f32[8,8,16,128]{3,2,1,0:T(8,128)S(1)} %all_to_all.10.own_ref), custom_call_target="tpu_custom_call" | custom-call | flops 182452224 | bytes 524288 | tf_op jit(solution)/shard_map/look_own/pallas_call | solution.py:136
  17.0 8.4 %collective-permute-done.later_ref = f32[5,8,16,128]{3,2,1,0:T(8,128)S(1)} collective-permute-done((f32[5,8,16,128]{3,2,1,0:T(8,128)S(1)}, f32[5,8,16,128]{3,2,1,0:T(8,128)S(1)}, u32[]{:S(2)}, u32[]{:S(2)}) %collective-permute-start) | collective-permute-done | bytes 327712 | tf_op jit(solution)/shard_map/ppermute | solution.py:236
  25.4 0.4 look_later.1
  25.8 16.6 %all_to_all.11 = f32[32,16,128]{2,1,0:T(8,128)S(1)} all-to-all(f32[32,16,128]{2,1,0:T(8,128)S(1)} %bitcast.6), channel_id=1, replica_groups={{0,1,2,3,4,5,6,7,8,9,10,11,12,13,14,15,16,17,18,19,20,21,22,23,24,25,26..., dimensions={0} | all-to-all | bytes 524288 | tf_op jit(solution)/shard_map/all_to_all | solution.py:239
  42.4 0.8 %finish.1 = (f32[5,2,1,8,128]{4,3,2,1,0:T(8,128)}, f32[5,1,8,128]{3,2,1,0:T(8,128)}) custom-call(f32[512,128]{1,0:T(8,128)S(1)} %bitcast.5), custom_call_target="tpu_custom_call" | custom-call | tf_op jit(solution)/shard_map/finish/pallas_call | solution.py:212
  (1 shorter events, 0.0 us)
Async XLA Ops:
  15.3 10.1 %collective-permute-start = (f32[5,8,16,128]{3,2,1,0:T(8,128)S(1)}, f32[5,8,16,128]{3,2,1,0:T(8,128)S(1)}, u32[]{:S(2)}, u32[]{:S(2)}) collective-permute-start(f32[5,8,16,128]{3,2,1,0:T(8,128)S(1)} %slice.4), channel_id=1, source_target_pairs={{32,0},{36,4},{40,8},{44,12},{48,16},{52,20},{56,24},{60,28},{64,3... | collective-permute-start | bytes 983048 | tf_op jit(solution)/shard_map/ppermute | solution.py:236
where the time goes:
time: 43.8 us; the launch traced here: 43.2 us
  blocking collectives  29.9 us (68%)
  waiting for transfers between devices  8.37 us (19%)
  Pallas kernels  2.95 us (7%)
  starting transfers between devices  1.29 us (3%)
  between operations  0.66 us (2%)
    all_to_all x1, blocking collectives, local(): lax.all_to_all(fields, ('date', 'az'), 0, 0, axis_index_groups=wide, tile...  16.6 us
    all_to_all x1, blocking collectives, local(): lax.all_to_all(pieces, 'date', 0, 0, axis_index_groups=groups, tiled=True)  13.3 us
    ppermute x1, waiting for transfers between devices, local(): later = lax.ppermute(own[:SPAN], 'date', back)  8.37 us
    pallas_call x1, Pallas kernels, cut(): pl.pallas_call(cut_kernel, in_specs=[pl.BlockSpec(memory_space=pl.ANY)],...  1.33 us
    ppermute x1, starting transfers between devices, local(): later = lax.ppermute(own[:SPAN], 'date', back)  1.29 us
  transfers between devices with their start and end apart: 1, of which 1 were waited for; matrix products, arithmetic and copies ran while one was open for 0% of the time, Pallas kernels for 1%

commit v1 on v0

--- a/solution.py
+++ b/solution.py
@@ -19,19 +19,18 @@
 def cut_kernel(slab_ref, out_ref, held, arrived):
     planes, lines, _ = slab_ref.shape
     width = out_ref.shape[-1]
-    blocks = SUB // 2
-    parts = [(p, line, b) for line in range(0, lines, 8) for p in range(planes) for b in range(0, SUB, blocks)]
     copies = []
-    for plane, line, first in parts:
-        here = (plane, pl.ds(line, 8), pl.ds(first * width, blocks * width))
+    for line in range(0, lines, 8):
+        here = (pl.ds(0, planes), pl.ds(line, 8))
         copies.append(pltpu.make_async_copy(slab_ref.at[here], held.at[here], arrived.at[len(copies)]))
-        copies[-1].start(priority=first // blocks)
-    for (plane, line, first), copy in zip(parts, copies):
+        copies[-1].start()
+    for line, copy in zip(range(0, lines, 8), copies):
         copy.wait()
-        for block in range(first, first + blocks):
-            part = held[plane, line : line + 8, block * width : (block + 1) * width]
-            start = (line * planes + plane) * SUB + block
-            out_ref[pl.ds(start, 8, stride=planes * SUB), :] = part
+        for plane in range(planes):
+            for block in range(SUB):
+                part = held[plane, line : line + 8, block * width : (block + 1) * width]
+                start = (line * planes + plane) * SUB + block
+                out_ref[pl.ds(start, 8, stride=planes * SUB), :] = part
 
 
 def cut(slab):
@@ -44,7 +43,7 @@
         out_shape=jax.ShapeDtypeStruct((rows, samples // SUB), jnp.float32),
         scratch_shapes=[
             pltpu.VMEM(slab.shape, jnp.float32),
-            pltpu.SemaphoreType.DMA((planes * lines // 4,)),
+            pltpu.SemaphoreType.DMA((lines // 8,)),
         ],
         compiler_params=pltpu.CompilerParams(vmem_limit_bytes=4 * 1024 * 1024),
         name="cut",
@@ -160,7 +159,7 @@
     )(own, later, looks)
 
 
-def coherence_kernel(tiles, rows_ref, looks_out, coher_out, looks_ref, values, coher_ref, sent):
+def coherence_kernel(tiles, rows_ref, looks_out, coher_out, looks_ref, boxes, coher_ref, sent):
     date, dates = lax.axis_index("date"), lax.axis_size("date")
     tile = lax.axis_index("az")
     cols = rows_ref.shape[-1]
@@ -190,14 +189,12 @@
         for shift in range(1, half + 1):
             boxed = boxed + jnp.where(lane >= shift, pltpu.roll(tall, shift, 1), 0.0)
             boxed = boxed + jnp.where(lane < cols - shift, pltpu.roll(tall, cols - shift, 1), 0.0)
-        real = boxed[:SPAN]
-        imag = boxed[SPAN : 2 * SPAN]
-        own = boxed[2 * SPAN : 2 * SPAN + 1]
-        later = boxed[2 * SPAN + 1 :]
-        value = jnp.sqrt(real * real + imag * imag) / jnp.sqrt(own * later + 1e-06)
-        values[r * GROUP : r * GROUP + SPAN, :] = value
+        boxes[r * FIELDS : (r + 1) * FIELDS, :] = boxed
+    fields = [boxes[pl.ds(field, GROUP, stride=FIELDS), :] for field in range(FIELDS)]
+    own, later = fields[2 * SPAN], fields[2 * SPAN + 1 :]
     for gap in range(1, SPAN + 1):
-        value = values[pl.ds(gap - 1, GROUP, stride=GROUP), :]
+        real, imag = fields[gap - 1], fields[SPAN + gap - 1]
+        value = jnp.sqrt(real * real + imag * imag) / jnp.sqrt(own * later[gap - 1] + 1e-06)
         coher_ref[gap - 1, 0] = jnp.where(date + gap < dates, value, 0.0)
     coher_sent = pltpu.make_async_copy(coher_ref, coher_out, sent.at[1])
     coher_sent.start()
@@ -215,7 +212,7 @@
         out_specs=(pl.BlockSpec(memory_space=pl.ANY), pl.BlockSpec(memory_space=pl.ANY)),
         scratch_shapes=[
             pltpu.VMEM(looks, jnp.float32),
-            pltpu.VMEM((GROUP * GROUP, cols), jnp.float32),
+            pltpu.VMEM((GROUP * FIELDS, cols), jnp.float32),
             pltpu.VMEM(coher, jnp.float32),
             pltpu.SemaphoreType.DMA((2,)),
         ],

time: 43.8 us -> 43.7 us (level)
  no operation moved by 1% of the time
where the time goes in v1:
time: 43.7 us; the launch traced here: 43.1 us
  blocking collectives  29.9 us (68%)
  waiting for transfers between devices  8.37 us (19%)
  Pallas kernels  2.88 us (7%)
  starting transfers between devices  1.29 us (3%)
  between operations  0.66 us (2%)
    all_to_all x1, blocking collectives, local(): lax.all_to_all(fields, ('date', 'az'), 0, 0, axis_index_groups=wide, tile...  16.6 us
    all_to_all x1, blocking collectives, local(): lax.all_to_all(pieces, 'date', 0, 0, axis_index_groups=groups, tiled=True)  13.3 us
    ppermute x1, waiting for transfers between devices, local(): later = lax.ppermute(own[:SPAN], 'date', back)  8.37 us
    ppermute x1, starting transfers between devices, local(): later = lax.ppermute(own[:SPAN], 'date', back)  1.29 us
    pallas_call x1, Pallas kernels, cut(): pl.pallas_call(cut_kernel, in_specs=[pl.BlockSpec(memory_space=pl.ANY)],...  1.26 us
  transfers between devices with their start and end apart: 1, of which 1 were waited for; matrix products, arithmetic and copies ran while one was open for 0% of the time, Pallas kernels for 1%

profile of v1, /device:TPU:1, one launch (start us, length us, event | category | flops | bytes accessed | tf_op | source)
XLA Modules:
  0.0 43.1 jit_solution(13523731786895424052)
XLA Ops:
  0.6 1.3 %cut.1 = f32[1024,128]{1,0:T(8,128)S(1)} custom-call(f32[2,32,2048]{2,1,0:T(8,128)} %bitcast.7), custom_call_target="tpu_custom_call" | custom-call | tf_op jit(solution)/shard_map/cut/pallas_call | solution.py:40
  1.9 13.3 %all_to_all.10.own_ref = f32[8,8,16,128]{3,2,1,0:T(8,128)S(1)} all-to-all(f32[8,8,16,128]{3,2,1,0:T(8,128)S(1)} %bitcast.4), channel_id=1, replica_groups={{0,4,8,12,16,20,24,28},{32,36,40,44,48,52,56,60},{64,68,72,76,80,84,88,..., dimensions={0} | all-to-all | bytes 1048576 | tf_op jit(solution)/shard_map/all_to_all | solution.py:231
  15.2 1.3 %collective-permute-start = (f32[5,8,16,128]{3,2,1,0:T(8,128)S(1)}, f32[5,8,16,128]{3,2,1,0:T(8,128)S(1)}, u32[]{:S(2)}, u32[]{:S(2)}) collective-permute-start(f32[5,8,16,128]{3,2,1,0:T(8,128)S(1)} %slice.4), channel_id=1, source_target_pairs={{32,0},{36,4},{40,8},{44,12},{48,16},{52,20},{56,24},{60,28},{64,3... | collective-permute-start | bytes 983048 | tf_op jit(solution)/shard_map/ppermute | solution.py:233
  16.5 0.5 %look_own.1.looks_ref = f32[58,128]{1,0:T(8,128)S(1)} custom-call(f32[8,8,16,128]{3,2,1,0:T(8,128)S(1)} %all_to_all.10.own_ref), custom_call_target="tpu_custom_call" | custom-call | flops 182452224 | bytes 524288 | tf_op jit(solution)/shard_map/look_own/pallas_call | solution.py:135
  17.0 8.4 %collective-permute-done.later_ref = f32[5,8,16,128]{3,2,1,0:T(8,128)S(1)} collective-permute-done((f32[5,8,16,128]{3,2,1,0:T(8,128)S(1)}, f32[5,8,16,128]{3,2,1,0:T(8,128)S(1)}, u32[]{:S(2)}, u32[]{:S(2)}) %collective-permute-start) | collective-permute-done | bytes 327712 | tf_op jit(solution)/shard_map/ppermute | solution.py:233
  25.3 0.4 look_later.1
  25.7 16.6 %all_to_all.11 = f32[32,16,128]{2,1,0:T(8,128)S(1)} all-to-all(f32[32,16,128]{2,1,0:T(8,128)S(1)} %bitcast.6), channel_id=1, replica_groups={{0,1,2,3,4,5,6,7,8,9,10,11,12,13,14,15,16,17,18,19,20,21,22,23,24,25,26..., dimensions={0} | all-to-all | bytes 524288 | tf_op jit(solution)/shard_map/all_to_all | solution.py:236
  42.3 0.8 %finish.1 = (f32[5,2,1,8,128]{4,3,2,1,0:T(8,128)}, f32[5,1,8,128]{3,2,1,0:T(8,128)}) custom-call(f32[512,128]{1,0:T(8,128)S(1)} %bitcast.5), custom_call_target="tpu_custom_call" | custom-call | tf_op jit(solution)/shard_map/finish/pallas_call | solution.py:209
  (1 shorter events, 0.0 us)
Async XLA Ops:
  15.2 10.1 %collective-permute-start = (f32[5,8,16,128]{3,2,1,0:T(8,128)S(1)}, f32[5,8,16,128]{3,2,1,0:T(8,128)S(1)}, u32[]{:S(2)}, u32[]{:S(2)}) collective-permute-start(f32[5,8,16,128]{3,2,1,0:T(8,128)S(1)} %slice.4), channel_id=1, source_target_pairs={{32,0},{36,4},{40,8},{44,12},{48,16},{52,20},{56,24},{60,28},{64,3... | collective-permute-start | bytes 983048 | tf_op jit(solution)/shard_map/ppermute | solution.py:233

commit v2 on v1

--- a/solution.py
+++ b/solution.py
@@ -97,6 +97,17 @@
     return [ref[at, 2 * k] for k in range(LOOK_AZ)], [ref[at, 2 * k + 1] for k in range(LOOK_AZ)]
 
 
+FIRST = GROUP - SPAN
+
+
+def order(tile):
+    return [(d + FIRST * (tile % 2)) % GROUP for d in range(GROUP)]
+
+
+def is_odd():
+    return lax.rem(lax.axis_index("az"), 2) == 1
+
+
 OWN_PAIRS = [(d, range(1, inside(d) + 1)) for d in range(GROUP)]
 LATER_PAIRS = [(d, range(inside(d) + 1, SPAN + 1)) for d in range(GROUP) if inside(d) < SPAN]
 OWN_ROWS = sum(2 * len(gaps) for _, gaps in OWN_PAIRS)
@@ -104,18 +115,36 @@
 
 
 def own_kernel(own_ref, out_ref, sums):
-    out_ref[...] = look_at(lambda d: planes_of(own_ref, d), OWN_PAIRS, range(GROUP), sums, out_ref.shape[-1])
-
-
-def later_kernel(own_ref, later_ref, looks_ref, out_ref, sums, cells):
+    shift = jnp.where(is_odd(), GROUP - FIRST, 0)
+
     def date(index):
-        return planes_of(own_ref, index) if index < GROUP else planes_of(later_ref, index - GROUP)
-
-    cells[...] = look_at(date, LATER_PAIRS, range(GROUP, GROUP + SPAN), sums, out_ref.shape[-1])
+        return planes_of(own_ref, lax.rem(index + shift, GROUP))
+
+    out_ref[...] = look_at(date, OWN_PAIRS, range(GROUP), sums, out_ref.shape[-1])
+
+
+def cross_kernel(own_ref, other_ref, out_ref, sums):
+    odd = is_odd()
+
+    def even_date(index):
+        return planes_of(own_ref, index) if index < GROUP else planes_of(other_ref, index - GROUP)
+
+    def odd_date(index):
+        return planes_of(other_ref, index - FIRST) if index < GROUP else planes_of(own_ref, (index - FIRST) % GROUP)
+
+    for date, here in ((even_date, jnp.logical_not(odd)), (odd_date, odd)):
+
+        @pl.when(here)
+        def _(date=date):
+            out_ref[...] = look_at(date, LATER_PAIRS, range(GROUP, GROUP + SPAN), sums, out_ref.shape[-1])
+
+
+def join_kernel(looks_ref, here_ref, back_ref, out_ref, cells):
+    cells[...] = jnp.where(is_odd(), back_ref[...], here_ref[...])
     own_at = later_at = 0
     for index in range(GROUP):
         near, far = inside(index), SPAN - inside(index)
-        piece = out_ref.at[index, 0]
+        piece = out_ref.at[0, index]
         for part in range(2):
             if near:
                 piece[part * SPAN : part * SPAN + near, :] = looks_ref[own_at : own_at + near, :]
@@ -126,8 +155,9 @@
         piece[2 * SPAN : 2 * SPAN + 1 + near, :] = looks_ref[OWN_ROWS + index : OWN_ROWS + index + 1 + near, :]
         if far:
             piece[2 * SPAN + 1 + near :, :] = cells[LATER_ROWS : LATER_ROWS + far, :]
-        for tile in range(1, out_ref.shape[1]):
-            out_ref[index, tile] = out_ref[index, 0]
+    for tile in range(1, out_ref.shape[0]):
+        for place, index in enumerate(order(tile)):
+            out_ref[tile, place] = out_ref[0, index]
 
 
 def look_own(own, cols):
@@ -144,19 +174,25 @@
     )(own)
 
 
-def look_later(own, later, looks, tiles):
-    cols = looks.shape[-1]
+def look_across(own, other, cols):
     rows = LATER_ROWS + SPAN
     return pl.pallas_call(
-        later_kernel,
-        out_shape=jax.ShapeDtypeStruct((GROUP, tiles, FIELDS, cols), jnp.float32),
-        scratch_shapes=[
-            pltpu.VMEM((rows * SUB, own.shape[-1]), jnp.float32),
-            pltpu.VMEM((rows, cols), jnp.float32),
-        ],
+        cross_kernel,
+        out_shape=jax.ShapeDtypeStruct((rows, cols), jnp.float32),
+        scratch_shapes=[pltpu.VMEM((rows * SUB, own.shape[-1]), jnp.float32)],
         compiler_params=pltpu.CompilerParams(vmem_limit_bytes=8 * 1024 * 1024),
-        name="look_later",
-    )(own, later, looks)
+        name="look_across",
+    )(own, other)
+
+
+def join(looks, here, back, tiles):
+    return pl.pallas_call(
+        join_kernel,
+        out_shape=jax.ShapeDtypeStruct((tiles, GROUP, FIELDS, looks.shape[-1]), jnp.float32),
+        scratch_shapes=[pltpu.VMEM(here.shape, jnp.float32)],
+        compiler_params=pltpu.CompilerParams(vmem_limit_bytes=4 * 1024 * 1024),
+        name="join",
+    )(looks, here, back)
 
 
 def coherence_kernel(tiles, rows_ref, looks_out, coher_out, looks_ref, boxes, coher_ref, sent):
@@ -166,8 +202,8 @@
     half = WIN // 2
     for gap in range(1, SPAN + 1):
         for part in range(2):
-            start = tile * FIELDS + part * SPAN + gap - 1
-            look = rows_ref[pl.ds(start, GROUP, stride=tiles * FIELDS), :]
+            start = tile * (GROUP * FIELDS) + part * SPAN + gap - 1
+            look = rows_ref[pl.ds(start, GROUP, stride=FIELDS), :]
             looks_ref[gap - 1, part, 0] = jnp.where(date + gap < dates, look, 0.0)
     looks_sent = pltpu.make_async_copy(looks_ref, looks_out, sent.at[0])
     looks_sent.start()
@@ -176,7 +212,7 @@
     rows = []
     for offset in range(-half, GROUP + half):
         other = tile + offset // GROUP
-        start = (offset % GROUP * tiles + jnp.clip(other, 0, tiles - 1)) * FIELDS
+        start = (jnp.clip(other, 0, tiles - 1) * GROUP + offset % GROUP) * FIELDS
         row = rows_ref[pl.ds(pl.multiple_of(start, FIELDS), FIELDS), :]
         if not 0 <= offset < GROUP:
             row = jnp.where(jnp.logical_and(other >= 0, other < tiles), row, 0.0)
@@ -225,13 +261,19 @@
     dates, tiles = lax.axis_size("date"), lax.axis_size("az")
     _, planes, lines, samples = slabs.shape
     cols = samples // LOOK_RG
-    groups = [list(range(g, g + GROUP)) for g in range(0, dates, GROUP)]
-    wide = [list(range(g * tiles, (g + GROUP) * tiles)) for g in range(0, dates, GROUP)]
+    both = ("date", "az")
+    starts = range(0, dates, GROUP)
+    groups = [[(g + d) * tiles + a for d in order(a)] for g in starts for a in range(tiles)]
+    wide = [[(g + d) * tiles + a for a in range(tiles) for d in order(a)] for g in starts]
+    down = [((d + GROUP) * tiles + a, d * tiles + a) for d in range(dates - GROUP) for a in range(tiles)]
+    across = [pair if pair[0] % tiles % 2 == 0 else pair[::-1] for pair in down]
+    home = [pair for pair in down if pair[0] % tiles % 2]
     pieces = cut(slabs[0]).reshape(GROUP, LOOK_AZ * planes, SUB, samples // SUB)
-    own = lax.all_to_all(pieces, "date", 0, 0, axis_index_groups=groups, tiled=True)
-    back = [(i, i - GROUP) for i in range(GROUP, dates)]
-    later = lax.ppermute(own[:SPAN], "date", back)
-    fields = look_later(own, later, look_own(own, cols), tiles)
+    own = lax.all_to_all(pieces, both, 0, 0, axis_index_groups=groups, tiled=True)
+    other = lax.ppermute(own[:SPAN], both, across)
+    looks = look_own(own, cols)
+    here = look_across(own, other, cols)
+    fields = join(looks, here, lax.ppermute(here, both, home), tiles)
     fields = fields.reshape(GROUP * tiles, FIELDS, cols)
     rows = lax.all_to_all(fields, ("date", "az"), 0, 0, axis_index_groups=wide, tiled=True)
     return finish(rows.reshape(GROUP * tiles * FIELDS, cols), tiles)

time: 43.7 us -> 45.4 us (1.039)
  the two profiles are of different devices: /device:TPU:1 before, /device:TPU:97 now
where the time goes in v2:
time: 45.4 us; the launch traced here: 45.1 us
  blocking collectives  27.1 us (60%)
  waiting for transfers between devices  7.79 us (17%)
  starting transfers between devices  6.68 us (15%)
  Pallas kernels  2.89 us (6%)
  between operations  0.67 us (1%)
    all_to_all x1, blocking collectives, local(): lax.all_to_all(fields, ('date', 'az'), 0, 0, axis_index_groups=wide, tile...  14.6 us
    all_to_all x1, blocking collectives, local(): lax.all_to_all(pieces, both, 0, 0, axis_index_groups=groups, tiled=True)  12.5 us
    ppermute x1, starting transfers between devices, local(): other = lax.ppermute(own[:SPAN], both, across)  4.76 us
    ppermute x1, waiting for transfers between devices, local(): other = lax.ppermute(own[:SPAN], both, across)  4 us
    ppermute x1, waiting for transfers between devices, local(): fields = join(looks, here, lax.ppermute(here, both, home), tiles)  3.8 us
    ppermute x1, starting transfers between devices, local(): fields = join(looks, here, lax.ppermute(here, both, home), tiles)  1.92 us
    pallas_call x1, Pallas kernels, cut(): pl.pallas_call(cut_kernel, in_specs=[pl.BlockSpec(memory_space=pl.ANY)],...  1.26 us
  transfers between devices with their start and end apart: 2, of which 2 were waited for; matrix products, arithmetic and copies ran while one was open for 0% of the time, Pallas kernels for 1%

profile of v2, /device:TPU:97, one launch (start us, length us, event | category | flops | bytes accessed | tf_op | source)
XLA Modules:
  0.0 45.1 jit_solution(6036522030720936566)
XLA Ops:
  0.6 1.3 %cut.1 = f32[1024,128]{1,0:T(8,128)S(1)} custom-call(f32[2,32,2048]{2,1,0:T(8,128)} %bitcast.7), custom_call_target="tpu_custom_call" | custom-call | tf_op jit(solution)/shard_map/cut/pallas_call | solution.py:40
  1.9 12.5 %all_to_all.10.own_ref = f32[8,8,16,128]{3,2,1,0:T(8,128)S(1)} all-to-all(f32[8,8,16,128]{3,2,1,0:T(8,128)S(1)} %bitcast.4), channel_id=1, replica_groups={{0,4,8,12,16,20,24,28},{13,17,21,25,29,1,5,9},{2,6,10,14,18,22,26,30},{..., dimensions={0} | all-to-all | bytes 1048576 | tf_op jit(solution)/shard_map/all_to_all | solution.py:272
  14.4 4.8 %collective-permute-start = (f32[5,8,16,128]{3,2,1,0:T(8,128)S(1)}, f32[5,8,16,128]{3,2,1,0:T(8,128)S(1)}, u32[]{:S(2)}, u32[]{:S(2)}) collective-permute-start(f32[5,8,16,128]{3,2,1,0:T(8,128)S(1)} %slice.4), channel_id=1, source_target_pairs={{32,0},{1,33},{34,2},{3,35},{36,4},{5,37},{38,6},{7,39},{40,8},{9,... | collective-permute-start | bytes 983048 | tf_op jit(solution)/shard_map/ppermute | solution.py:273
  19.2 4.0 %collective-permute-done.other_ref = f32[5,8,16,128]{3,2,1,0:T(8,128)S(1)} collective-permute-done((f32[5,8,16,128]{3,2,1,0:T(8,128)S(1)}, f32[5,8,16,128]{3,2,1,0:T(8,128)S(1)}, u32[]{:S(2)}, u32[]{:S(2)}) %collective-permute-start) | collective-permute-done | bytes 327712 | tf_op jit(solution)/shard_map/ppermute | solution.py:273
  23.2 0.3 look_across.1.here_ref
  23.5 1.9 %collective-permute-start.1 = (f32[35,128]{1,0:T(8,128)S(1)}, f32[35,128]{1,0:T(8,128)S(1)}, u32[]{:S(2)}, u32[]{:S(2)}) collective-permute-start(f32[35,128]{1,0:T(8,128)S(1)} %look_across.1.here_ref), channel_id=1, source_target_pairs={{33,1},{35,3},{37,5},{39,7},{41,9},{43,11},{45,13},{47,15},{49,17}... | collective-permute-start | bytes 53768 | tf_op jit(solution)/shard_map/ppermute | solution.py:276
  25.5 0.5 %look_own.1.looks_ref = f32[58,128]{1,0:T(8,128)S(1)} custom-call(f32[8,8,16,128]{3,2,1,0:T(8,128)S(1)} %all_to_all.10.own_ref), custom_call_target="tpu_custom_call" | custom-call | flops 182452224 | bytes 524288 | tf_op jit(solution)/shard_map/look_own/pallas_call | solution.py:165
  25.9 3.8 %collective-permute-done.1.back_ref = f32[35,128]{1,0:T(8,128)S(1)} collective-permute-done((f32[35,128]{1,0:T(8,128)S(1)}, f32[35,128]{1,0:T(8,128)S(1)}, u32[]{:S(2)}, u32[]{:S(2)}) %collective-permute-start.1) | collective-permute-done | bytes 17952 | tf_op jit(solution)/shard_map/ppermute | solution.py:276
  29.8 14.6 %all_to_all.11 = f32[32,16,128]{2,1,0:T(8,128)S(1)} all-to-all(f32[32,16,128]{2,1,0:T(8,128)S(1)} %bitcast.5), channel_id=1, replica_groups={{0,4,8,12,16,20,24,28,13,17,21,25,29,1,5,9,2,6,10,14,18,22,26,30,15,19,..., dimensions={0} | all-to-all | bytes 524288 | tf_op jit(solution)/shard_map/all_to_all | solution.py:278
  44.4 0.8 %finish.1 = (f32[5,2,1,8,128]{4,3,2,1,0:T(8,128)}, f32[5,1,8,128]{3,2,1,0:T(8,128)}) custom-call(f32[512,128]{1,0:T(8,128)S(1)} %bitcast.6), custom_call_target="tpu_custom_call" | custom-call | tf_op jit(solution)/shard_map/finish/pallas_call | solution.py:245
  (2 shorter events, 0.1 us)
Async XLA Ops:
  14.4 8.8 %collective-permute-start = (f32[5,8,16,128]{3,2,1,0:T(8,128)S(1)}, f32[5,8,16,128]{3,2,1,0:T(8,128)S(1)}, u32[]{:S(2)}, u32[]{:S(2)}) collective-permute-start(f32[5,8,16,128]{3,2,1,0:T(8,128)S(1)} %slice.4), channel_id=1, source_target_pairs={{32,0},{1,33},{34,2},{3,35},{36,4},{5,37},{38,6},{7,39},{40,8},{9,... | collective-permute-start | bytes 983048 | tf_op jit(solution)/shard_map/ppermute | solution.py:273
  23.5 6.2 %collective-permute-start.1 = (f32[35,128]{1,0:T(8,128)S(1)}, f32[35,128]{1,0:T(8,128)S(1)}, u32[]{:S(2)}, u32[]{:S(2)}) collective-permute-start(f32[35,128]{1,0:T(8,128)S(1)} %look_across.1.here_ref), channel_id=1, source_target_pairs={{33,1},{35,3},{37,5},{39,7},{41,9},{43,11},{45,13},{47,15},{49,17}... | collective-permute-start | bytes 53768 | tf_op jit(solution)/shard_map/ppermute | solution.py:276

commit v3 on v1

--- a/solution.py
+++ b/solution.py
@@ -104,18 +104,21 @@
 
 
 def own_kernel(own_ref, out_ref, sums):
-    out_ref[...] = look_at(lambda d: planes_of(own_ref, d), OWN_PAIRS, range(GROUP), sums, out_ref.shape[-1])
+    out_ref[...] = look_at(lambda d: planes_of(own_ref, GROUP - 1 - d), OWN_PAIRS, range(GROUP), sums, out_ref.shape[-1])
 
 
 def later_kernel(own_ref, later_ref, looks_ref, out_ref, sums, cells):
     def date(index):
-        return planes_of(own_ref, index) if index < GROUP else planes_of(later_ref, index - GROUP)
+        if index < GROUP:
+            return planes_of(own_ref, GROUP - 1 - index)
+        return planes_of(later_ref, GROUP + SPAN - 1 - index)
 
     cells[...] = look_at(date, LATER_PAIRS, range(GROUP, GROUP + SPAN), sums, out_ref.shape[-1])
     own_at = later_at = 0
     for index in range(GROUP):
         near, far = inside(index), SPAN - inside(index)
-        piece = out_ref.at[index, 0]
+        place = GROUP - 1 - index
+        piece = out_ref.at[place, 0]
         for part in range(2):
             if near:
                 piece[part * SPAN : part * SPAN + near, :] = looks_ref[own_at : own_at + near, :]
@@ -127,7 +130,7 @@
         if far:
             piece[2 * SPAN + 1 + near :, :] = cells[LATER_ROWS : LATER_ROWS + far, :]
         for tile in range(1, out_ref.shape[1]):
-            out_ref[index, tile] = out_ref[index, 0]
+            out_ref[place, tile] = out_ref[place, 0]
 
 
 def look_own(own, cols):
@@ -225,12 +228,12 @@
     dates, tiles = lax.axis_size("date"), lax.axis_size("az")
     _, planes, lines, samples = slabs.shape
     cols = samples // LOOK_RG
-    groups = [list(range(g, g + GROUP)) for g in range(0, dates, GROUP)]
-    wide = [list(range(g * tiles, (g + GROUP) * tiles)) for g in range(0, dates, GROUP)]
+    groups = [list(range(g, g + GROUP))[::-1] for g in range(0, dates, GROUP)]
+    wide = [[d * tiles + a for d in group for a in range(tiles)] for group in groups]
     pieces = cut(slabs[0]).reshape(GROUP, LOOK_AZ * planes, SUB, samples // SUB)
     own = lax.all_to_all(pieces, "date", 0, 0, axis_index_groups=groups, tiled=True)
     back = [(i, i - GROUP) for i in range(GROUP, dates)]
-    later = lax.ppermute(own[:SPAN], "date", back)
+    later = lax.ppermute(own[GROUP - SPAN :], "date", back)
     fields = look_later(own, later, look_own(own, cols), tiles)
     fields = fields.reshape(GROUP * tiles, FIELDS, cols)
     rows = lax.all_to_all(fields, ("date", "az"), 0, 0, axis_index_groups=wide, tiled=True)

time: 43.7 us -> 42.5 us (0.973)
  blocking collectives: 29.9 us -> 28.9 us
    all_to_all x1, blocking collectives: 13.3 us -> 12 us  [local(): lax.all_to_all(pieces, 'date', 0, 0, axis_index_groups=groups, tiled=True)]
where the time goes in v3:
time: 42.5 us; the launch traced here: 42 us
  blocking collectives  28.9 us (68%)
  waiting for transfers between devices  8.25 us (19%)
  Pallas kernels  2.88 us (7%)
  starting transfers between devices  1.29 us (3%)
  between operations  0.66 us (2%)
    all_to_all x1, blocking collectives, local(): lax.all_to_all(fields, ('date', 'az'), 0, 0, axis_index_groups=wide, tile...  16.9 us
    all_to_all x1, blocking collectives, local(): lax.all_to_all(pieces, 'date', 0, 0, axis_index_groups=groups, tiled=True)  12 us
    ppermute x1, waiting for transfers between devices, local(): later = lax.ppermute(own[GROUP - SPAN:], 'date', back)  8.25 us
    ppermute x1, starting transfers between devices, local(): later = lax.ppermute(own[GROUP - SPAN:], 'date', back)  1.29 us
    pallas_call x1, Pallas kernels, cut(): pl.pallas_call(cut_kernel, in_specs=[pl.BlockSpec(memory_space=pl.ANY)],...  1.26 us
  transfers between devices with their start and end apart: 1, of which 1 were waited for; matrix products, arithmetic and copies ran while one was open for 0% of the time, Pallas kernels for 1%

profile of v3, /device:TPU:1, one launch (start us, length us, event | category | flops | bytes accessed | tf_op | source)
XLA Modules:
  0.0 42.0 jit_solution(15855214702194791566)
XLA Ops:
  0.6 1.3 %cut.1 = f32[1024,128]{1,0:T(8,128)S(1)} custom-call(f32[2,32,2048]{2,1,0:T(8,128)} %bitcast.7), custom_call_target="tpu_custom_call" | custom-call | tf_op jit(solution)/shard_map/cut/pallas_call | solution.py:40
  1.9 12.0 %all_to_all.10.own_ref = f32[8,8,16,128]{3,2,1,0:T(8,128)S(1)} all-to-all(f32[8,8,16,128]{3,2,1,0:T(8,128)S(1)} %bitcast.4), channel_id=1, replica_groups={{28,24,20,16,12,8,4,0},{60,56,52,48,44,40,36,32},{92,88,84,80,76,72,68,..., dimensions={0} | all-to-all | bytes 1048576 | tf_op jit(solution)/shard_map/all_to_all | solution.py:234
  14.0 1.3 %collective-permute-start = (f32[5,8,16,128]{3,2,1,0:T(8,128)S(1)}, f32[5,8,16,128]{3,2,1,0:T(8,128)S(1)}, u32[]{:S(2)}, u32[]{:S(2)}) collective-permute-start(f32[5,8,16,128]{3,2,1,0:T(8,128)S(1)} %slice.4), channel_id=1, source_target_pairs={{32,0},{36,4},{40,8},{44,12},{48,16},{52,20},{56,24},{60,28},{64,3... | collective-permute-start | bytes 983048 | tf_op jit(solution)/shard_map/ppermute | solution.py:236
  15.3 0.5 %look_own.1.looks_ref = f32[58,128]{1,0:T(8,128)S(1)} custom-call(f32[8,8,16,128]{3,2,1,0:T(8,128)S(1)} %all_to_all.10.own_ref), custom_call_target="tpu_custom_call" | custom-call | flops 182452224 | bytes 524288 | tf_op jit(solution)/shard_map/look_own/pallas_call | solution.py:138
  15.7 8.2 %collective-permute-done.later_ref = f32[5,8,16,128]{3,2,1,0:T(8,128)S(1)} collective-permute-done((f32[5,8,16,128]{3,2,1,0:T(8,128)S(1)}, f32[5,8,16,128]{3,2,1,0:T(8,128)S(1)}, u32[]{:S(2)}, u32[]{:S(2)}) %collective-permute-start) | collective-permute-done | bytes 327712 | tf_op jit(solution)/shard_map/ppermute | solution.py:236
  24.0 0.4 look_later.1
  24.3 16.9 %all_to_all.11 = f32[32,16,128]{2,1,0:T(8,128)S(1)} all-to-all(f32[32,16,128]{2,1,0:T(8,128)S(1)} %bitcast.6), channel_id=1, replica_groups={{28,29,30,31,24,25,26,27,20,21,22,23,16,17,18,19,12,13,14,15,8,9,10,11,..., dimensions={0} | all-to-all | bytes 524288 | tf_op jit(solution)/shard_map/all_to_all | solution.py:239
  41.2 0.8 %finish.1 = (f32[5,2,1,8,128]{4,3,2,1,0:T(8,128)}, f32[5,1,8,128]{3,2,1,0:T(8,128)}) custom-call(f32[512,128]{1,0:T(8,128)S(1)} %bitcast.5), custom_call_target="tpu_custom_call" | custom-call | tf_op jit(solution)/shard_map/finish/pallas_call | solution.py:212
  (1 shorter events, 0.0 us)
Async XLA Ops:
  14.0 10.0 %collective-permute-start = (f32[5,8,16,128]{3,2,1,0:T(8,128)S(1)}, f32[5,8,16,128]{3,2,1,0:T(8,128)S(1)}, u32[]{:S(2)}, u32[]{:S(2)}) collective-permute-start(f32[5,8,16,128]{3,2,1,0:T(8,128)S(1)} %slice.4), channel_id=1, source_target_pairs={{32,0},{36,4},{40,8},{44,12},{48,16},{52,20},{56,24},{60,28},{64,3... | collective-permute-start | bytes 983048 | tf_op jit(solution)/shard_map/ppermute | solution.py:236

commit v4 on v3

--- a/solution.py
+++ b/solution.py
@@ -169,7 +169,7 @@
     half = WIN // 2
     for gap in range(1, SPAN + 1):
         for part in range(2):
-            start = tile * FIELDS + part * SPAN + gap - 1
+            start = (tiles - 1 - tile) * FIELDS + part * SPAN + gap - 1
             look = rows_ref[pl.ds(start, GROUP, stride=tiles * FIELDS), :]
             looks_ref[gap - 1, part, 0] = jnp.where(date + gap < dates, look, 0.0)
     looks_sent = pltpu.make_async_copy(looks_ref, looks_out, sent.at[0])
@@ -179,7 +179,7 @@
     rows = []
     for offset in range(-half, GROUP + half):
         other = tile + offset // GROUP
-        start = (offset % GROUP * tiles + jnp.clip(other, 0, tiles - 1)) * FIELDS
+        start = (offset % GROUP * tiles + tiles - 1 - jnp.clip(other, 0, tiles - 1)) * FIELDS
         row = rows_ref[pl.ds(pl.multiple_of(start, FIELDS), FIELDS), :]
         if not 0 <= offset < GROUP:
             row = jnp.where(jnp.logical_and(other >= 0, other < tiles), row, 0.0)
@@ -229,7 +229,7 @@
     _, planes, lines, samples = slabs.shape
     cols = samples // LOOK_RG
     groups = [list(range(g, g + GROUP))[::-1] for g in range(0, dates, GROUP)]
-    wide = [[d * tiles + a for d in group for a in range(tiles)] for group in groups]
+    wide = [[d * tiles + a for d in group for a in range(tiles)[::-1]] for group in groups]
     pieces = cut(slabs[0]).reshape(GROUP, LOOK_AZ * planes, SUB, samples // SUB)
     own = lax.all_to_all(pieces, "date", 0, 0, axis_index_groups=groups, tiled=True)
     back = [(i, i - GROUP) for i in range(GROUP, dates)]

time: 42.5 us -> 41.9 us (0.986)
  no operation moved by 1% of the time
where the time goes in v4:
time: 41.9 us; the launch traced here: 41.6 us
  blocking collectives  28.5 us (68%)
  waiting for transfers between devices  8.25 us (20%)
  Pallas kernels  2.88 us (7%)
  starting transfers between devices  1.29 us (3%)
  between operations  0.66 us (2%)
    all_to_all x1, blocking collectives, local(): lax.all_to_all(fields, ('date', 'az'), 0, 0, axis_index_groups=wide, tile...  16.5 us
    all_to_all x1, blocking collectives, local(): lax.all_to_all(pieces, 'date', 0, 0, axis_index_groups=groups, tiled=True)  12 us
    ppermute x1, waiting for transfers between devices, local(): later = lax.ppermute(own[GROUP - SPAN:], 'date', back)  8.25 us
    ppermute x1, starting transfers between devices, local(): later = lax.ppermute(own[GROUP - SPAN:], 'date', back)  1.29 us
    pallas_call x1, Pallas kernels, cut(): pl.pallas_call(cut_kernel, in_specs=[pl.BlockSpec(memory_space=pl.ANY)],...  1.26 us
  transfers between devices with their start and end apart: 1, of which 1 were waited for; matrix products, arithmetic and copies ran while one was open for 0% of the time, Pallas kernels for 1%

profile of v4, /device:TPU:1, one launch (start us, length us, event | category | flops | bytes accessed | tf_op | source)
XLA Modules:
  0.0 41.6 jit_solution(6302941633583936441)
XLA Ops:
  0.6 1.3 %cut.1 = f32[1024,128]{1,0:T(8,128)S(1)} custom-call(f32[2,32,2048]{2,1,0:T(8,128)} %bitcast.7), custom_call_target="tpu_custom_call" | custom-call | tf_op jit(solution)/shard_map/cut/pallas_call | solution.py:40
  1.9 12.0 %all_to_all.10.own_ref = f32[8,8,16,128]{3,2,1,0:T(8,128)S(1)} all-to-all(f32[8,8,16,128]{3,2,1,0:T(8,128)S(1)} %bitcast.4), channel_id=1, replica_groups={{28,24,20,16,12,8,4,0},{60,56,52,48,44,40,36,32},{92,88,84,80,76,72,68,..., dimensions={0} | all-to-all | bytes 1048576 | tf_op jit(solution)/shard_map/all_to_all | solution.py:234
  14.0 1.3 %collective-permute-start = (f32[5,8,16,128]{3,2,1,0:T(8,128)S(1)}, f32[5,8,16,128]{3,2,1,0:T(8,128)S(1)}, u32[]{:S(2)}, u32[]{:S(2)}) collective-permute-start(f32[5,8,16,128]{3,2,1,0:T(8,128)S(1)} %slice.4), channel_id=1, source_target_pairs={{32,0},{36,4},{40,8},{44,12},{48,16},{52,20},{56,24},{60,28},{64,3... | collective-permute-start | bytes 983048 | tf_op jit(solution)/shard_map/ppermute | solution.py:236
  15.3 0.5 %look_own.1.looks_ref = f32[58,128]{1,0:T(8,128)S(1)} custom-call(f32[8,8,16,128]{3,2,1,0:T(8,128)S(1)} %all_to_all.10.own_ref), custom_call_target="tpu_custom_call" | custom-call | flops 182452224 | bytes 524288 | tf_op jit(solution)/shard_map/look_own/pallas_call | solution.py:138
  15.7 8.2 %collective-permute-done.later_ref = f32[5,8,16,128]{3,2,1,0:T(8,128)S(1)} collective-permute-done((f32[5,8,16,128]{3,2,1,0:T(8,128)S(1)}, f32[5,8,16,128]{3,2,1,0:T(8,128)S(1)}, u32[]{:S(2)}, u32[]{:S(2)}) %collective-permute-start) | collective-permute-done | bytes 327712 | tf_op jit(solution)/shard_map/ppermute | solution.py:236
  24.0 0.4 look_later.1
  24.3 16.5 %all_to_all.11 = f32[32,16,128]{2,1,0:T(8,128)S(1)} all-to-all(f32[32,16,128]{2,1,0:T(8,128)S(1)} %bitcast.6), channel_id=1, replica_groups={{31,30,29,28,27,26,25,24,23,22,21,20,19,18,17,16,15,14,13,12,11,10,9,8,..., dimensions={0} | all-to-all | bytes 524288 | tf_op jit(solution)/shard_map/all_to_all | solution.py:239
  40.8 0.8 %finish.1 = (f32[5,2,1,8,128]{4,3,2,1,0:T(8,128)}, f32[5,1,8,128]{3,2,1,0:T(8,128)}) custom-call(f32[512,128]{1,0:T(8,128)S(1)} %bitcast.5), custom_call_target="tpu_custom_call" | custom-call | tf_op jit(solution)/shard_map/finish/pallas_call | solution.py:212
  (1 shorter events, 0.0 us)
Async XLA Ops:
  14.0 10.0 %collective-permute-start = (f32[5,8,16,128]{3,2,1,0:T(8,128)S(1)}, f32[5,8,16,128]{3,2,1,0:T(8,128)S(1)}, u32[]{:S(2)}, u32[]{:S(2)}) collective-permute-start(f32[5,8,16,128]{3,2,1,0:T(8,128)S(1)} %slice.4), channel_id=1, source_target_pairs={{32,0},{36,4},{40,8},{44,12},{48,16},{52,20},{56,24},{60,28},{64,3... | collective-permute-start | bytes 983048 | tf_op jit(solution)/shard_map/ppermute | solution.py:236

commit v5 on v4

--- a/solution.py
+++ b/solution.py
@@ -54,6 +54,10 @@
     return min(SPAN, GROUP - 1 - index)
 
 
+def at(tile, row, tiles):
+    return (tile % 2 * GROUP + row) * (tiles // 2) + tiles // 2 - 1 - tile // 2
+
+
 def look_at(date, pairs, powers, sums, cols):
     width = sums.shape[-1]
     count = 0
@@ -114,11 +118,12 @@
         return planes_of(later_ref, GROUP + SPAN - 1 - index)
 
     cells[...] = look_at(date, LATER_PAIRS, range(GROUP, GROUP + SPAN), sums, out_ref.shape[-1])
+    tiles = out_ref.shape[0] // GROUP
     own_at = later_at = 0
     for index in range(GROUP):
         near, far = inside(index), SPAN - inside(index)
         place = GROUP - 1 - index
-        piece = out_ref.at[place, 0]
+        piece = out_ref.at[at(0, place, tiles)]
         for part in range(2):
             if near:
                 piece[part * SPAN : part * SPAN + near, :] = looks_ref[own_at : own_at + near, :]
@@ -129,8 +134,8 @@
         piece[2 * SPAN : 2 * SPAN + 1 + near, :] = looks_ref[OWN_ROWS + index : OWN_ROWS + index + 1 + near, :]
         if far:
             piece[2 * SPAN + 1 + near :, :] = cells[LATER_ROWS : LATER_ROWS + far, :]
-        for tile in range(1, out_ref.shape[1]):
-            out_ref[place, tile] = out_ref[place, 0]
+        for tile in range(1, tiles):
+            out_ref[at(tile, place, tiles)] = out_ref[at(0, place, tiles)]
 
 
 def look_own(own, cols):
@@ -152,7 +157,7 @@
     rows = LATER_ROWS + SPAN
     return pl.pallas_call(
         later_kernel,
-        out_shape=jax.ShapeDtypeStruct((GROUP, tiles, FIELDS, cols), jnp.float32),
+        out_shape=jax.ShapeDtypeStruct((GROUP * tiles, FIELDS, cols), jnp.float32),
         scratch_shapes=[
             pltpu.VMEM((rows * SUB, own.shape[-1]), jnp.float32),
             pltpu.VMEM((rows, cols), jnp.float32),
@@ -169,8 +174,8 @@
     half = WIN // 2
     for gap in range(1, SPAN + 1):
         for part in range(2):
-            start = (tiles - 1 - tile) * FIELDS + part * SPAN + gap - 1
-            look = rows_ref[pl.ds(start, GROUP, stride=tiles * FIELDS), :]
+            start = at(tile, 0, tiles) * FIELDS + part * SPAN + gap - 1
+            look = rows_ref[pl.ds(start, GROUP, stride=tiles // 2 * FIELDS), :]
             looks_ref[gap - 1, part, 0] = jnp.where(date + gap < dates, look, 0.0)
     looks_sent = pltpu.make_async_copy(looks_ref, looks_out, sent.at[0])
     looks_sent.start()
@@ -179,7 +184,7 @@
     rows = []
     for offset in range(-half, GROUP + half):
         other = tile + offset // GROUP
-        start = (offset % GROUP * tiles + tiles - 1 - jnp.clip(other, 0, tiles - 1)) * FIELDS
+        start = at(jnp.clip(other, 0, tiles - 1), offset % GROUP, tiles) * FIELDS
         row = rows_ref[pl.ds(pl.multiple_of(start, FIELDS), FIELDS), :]
         if not 0 <= offset < GROUP:
             row = jnp.where(jnp.logical_and(other >= 0, other < tiles), row, 0.0)
@@ -229,13 +234,13 @@
     _, planes, lines, samples = slabs.shape
     cols = samples // LOOK_RG
     groups = [list(range(g, g + GROUP))[::-1] for g in range(0, dates, GROUP)]
-    wide = [[d * tiles + a for d in group for a in range(tiles)[::-1]] for group in groups]
+    places = sorted((at(a, row, tiles), row, a) for row in range(GROUP) for a in range(tiles))
+    wide = [[group[row] * tiles + a for _, row, a in places] for group in groups]
     pieces = cut(slabs[0]).reshape(GROUP, LOOK_AZ * planes, SUB, samples // SUB)
     own = lax.all_to_all(pieces, "date", 0, 0, axis_index_groups=groups, tiled=True)
     back = [(i, i - GROUP) for i in range(GROUP, dates)]
     later = lax.ppermute(own[GROUP - SPAN :], "date", back)
     fields = look_later(own, later, look_own(own, cols), tiles)
-    fields = fields.reshape(GROUP * tiles, FIELDS, cols)
     rows = lax.all_to_all(fields, ("date", "az"), 0, 0, axis_index_groups=wide, tiled=True)
     return finish(rows.reshape(GROUP * tiles * FIELDS, cols), tiles)
 

time: 41.9 us -> 42.5 us (1.014)
  blocking collectives: 28.5 us -> 29.2 us
    all_to_all x1, blocking collectives: 16.5 us -> 17.1 us  [local(): lax.all_to_all(fields, ('date', 'az'), 0, 0, axis_index_groups=wide, tile...]
where the time goes in v5:
time: 42.5 us; the launch traced here: 42.3 us
  blocking collectives  29.2 us (69%)
  waiting for transfers between devices  8.25 us (19%)
  Pallas kernels  2.88 us (7%)
  starting transfers between devices  1.29 us (3%)
  between operations  0.66 us (2%)
    all_to_all x1, blocking collectives, local(): lax.all_to_all(fields, ('date', 'az'), 0, 0, axis_index_groups=wide, tile...  17.1 us
    all_to_all x1, blocking collectives, local(): lax.all_to_all(pieces, 'date', 0, 0, axis_index_groups=groups, tiled=True)  12 us
    ppermute x1, waiting for transfers between devices, local(): later = lax.ppermute(own[GROUP - SPAN:], 'date', back)  8.25 us
    ppermute x1, starting transfers between devices, local(): later = lax.ppermute(own[GROUP - SPAN:], 'date', back)  1.29 us
    pallas_call x1, Pallas kernels, cut(): pl.pallas_call(cut_kernel, in_specs=[pl.BlockSpec(memory_space=pl.ANY)],...  1.26 us
  transfers between devices with their start and end apart: 1, of which 1 were waited for; matrix products, arithmetic and copies ran while one was open for 0% of the time, Pallas kernels for 1%

profile of v5, /device:TPU:1, one launch (start us, length us, event | category | flops | bytes accessed | tf_op | source)
XLA Modules:
  0.0 42.3 jit_solution(14202092403494212111)
XLA Ops:
  0.6 1.3 %cut.1 = f32[1024,128]{1,0:T(8,128)S(1)} custom-call(f32[2,32,2048]{2,1,0:T(8,128)} %bitcast.5), custom_call_target="tpu_custom_call" | custom-call | tf_op jit(solution)/shard_map/cut/pallas_call | solution.py:40
  1.9 12.0 %all_to_all.10.own_ref = f32[8,8,16,128]{3,2,1,0:T(8,128)S(1)} all-to-all(f32[8,8,16,128]{3,2,1,0:T(8,128)S(1)} %bitcast.3), channel_id=1, replica_groups={{28,24,20,16,12,8,4,0},{60,56,52,48,44,40,36,32},{92,88,84,80,76,72,68,..., dimensions={0} | all-to-all | bytes 1048576 | tf_op jit(solution)/shard_map/all_to_all | solution.py:240
  14.0 1.3 %collective-permute-start = (f32[5,8,16,128]{3,2,1,0:T(8,128)S(1)}, f32[5,8,16,128]{3,2,1,0:T(8,128)S(1)}, u32[]{:S(2)}, u32[]{:S(2)}) collective-permute-start(f32[5,8,16,128]{3,2,1,0:T(8,128)S(1)} %slice.4), channel_id=1, source_target_pairs={{32,0},{36,4},{40,8},{44,12},{48,16},{52,20},{56,24},{60,28},{64,3... | collective-permute-start | bytes 983048 | tf_op jit(solution)/shard_map/ppermute | solution.py:242
  15.3 0.5 %look_own.1.looks_ref = f32[58,128]{1,0:T(8,128)S(1)} custom-call(f32[8,8,16,128]{3,2,1,0:T(8,128)S(1)} %all_to_all.10.own_ref), custom_call_target="tpu_custom_call" | custom-call | flops 182452224 | bytes 524288 | tf_op jit(solution)/shard_map/look_own/pallas_call | solution.py:143
  15.7 8.2 %collective-permute-done.later_ref = f32[5,8,16,128]{3,2,1,0:T(8,128)S(1)} collective-permute-done((f32[5,8,16,128]{3,2,1,0:T(8,128)S(1)}, f32[5,8,16,128]{3,2,1,0:T(8,128)S(1)}, u32[]{:S(2)}, u32[]{:S(2)}) %collective-permute-start) | collective-permute-done | bytes 327712 | tf_op jit(solution)/shard_map/ppermute | solution.py:242
  24.0 0.4 look_later.1
  24.3 17.1 %all_to_all.11 = f32[32,16,128]{2,1,0:T(8,128)S(1)} all-to-all(f32[32,16,128]{2,1,0:T(8,128)S(1)} %look_later.1), channel_id=1, replica_groups={{30,28,26,24,22,20,18,16,14,12,10,8,6,4,2,0,31,29,27,25,23,21,19,17,15,..., dimensions={0} | all-to-all | bytes 524288 | tf_op jit(solution)/shard_map/all_to_all | solution.py:244
  41.5 0.8 %finish.1 = (f32[5,2,1,8,128]{4,3,2,1,0:T(8,128)}, f32[5,1,8,128]{3,2,1,0:T(8,128)}) custom-call(f32[512,128]{1,0:T(8,128)S(1)} %bitcast.4), custom_call_target="tpu_custom_call" | custom-call | tf_op jit(solution)/shard_map/finish/pallas_call | solution.py:217
  (1 shorter events, 0.0 us)
Async XLA Ops:
  14.0 10.0 %collective-permute-start = (f32[5,8,16,128]{3,2,1,0:T(8,128)S(1)}, f32[5,8,16,128]{3,2,1,0:T(8,128)S(1)}, u32[]{:S(2)}, u32[]{:S(2)}) collective-permute-start(f32[5,8,16,128]{3,2,1,0:T(8,128)S(1)} %slice.4), channel_id=1, source_target_pairs={{32,0},{36,4},{40,8},{44,12},{48,16},{52,20},{56,24},{60,28},{64,3... | collective-permute-start | bytes 983048 | tf_op jit(solution)/shard_map/ppermute | solution.py:242

commit v6 on v5

--- a/solution.py
+++ b/solution.py
@@ -13,6 +13,7 @@
 SPAN = 5
 GROUP = 8
 FIELDS = 3 * SPAN + 1
+ORDER = (5, 7, 6, 4, 3, 2, 1, 0)
 SUB = 16
 
 
@@ -108,21 +109,21 @@
 
 
 def own_kernel(own_ref, out_ref, sums):
-    out_ref[...] = look_at(lambda d: planes_of(own_ref, GROUP - 1 - d), OWN_PAIRS, range(GROUP), sums, out_ref.shape[-1])
+    out_ref[...] = look_at(lambda d: planes_of(own_ref, ORDER.index(d)), OWN_PAIRS, range(GROUP), sums, out_ref.shape[-1])
 
 
 def later_kernel(own_ref, later_ref, looks_ref, out_ref, sums, cells):
     def date(index):
         if index < GROUP:
-            return planes_of(own_ref, GROUP - 1 - index)
-        return planes_of(later_ref, GROUP + SPAN - 1 - index)
+            return planes_of(own_ref, ORDER.index(index))
+        return planes_of(later_ref, ORDER.index(index - GROUP) - (GROUP - SPAN))
 
     cells[...] = look_at(date, LATER_PAIRS, range(GROUP, GROUP + SPAN), sums, out_ref.shape[-1])
     tiles = out_ref.shape[0] // GROUP
     own_at = later_at = 0
     for index in range(GROUP):
         near, far = inside(index), SPAN - inside(index)
-        place = GROUP - 1 - index
+        place = ORDER.index(index)
         piece = out_ref.at[at(0, place, tiles)]
         for part in range(2):
             if near:
@@ -233,7 +234,7 @@
     dates, tiles = lax.axis_size("date"), lax.axis_size("az")
     _, planes, lines, samples = slabs.shape
     cols = samples // LOOK_RG
-    groups = [list(range(g, g + GROUP))[::-1] for g in range(0, dates, GROUP)]
+    groups = [[g + d for d in ORDER] for g in range(0, dates, GROUP)]
     places = sorted((at(a, row, tiles), row, a) for row in range(GROUP) for a in range(tiles))
     wide = [[group[row] * tiles + a for _, row, a in places] for group in groups]
     pieces = cut(slabs[0]).reshape(GROUP, LOOK_AZ * planes, SUB, samples // SUB)

time: 42.5 us -> 41.9 us (0.986)
  blocking collectives: 29.2 us -> 28.3 us
    all_to_all x1, blocking collectives: 12 us -> 11.1 us  [local(): lax.all_to_all(pieces, 'date', 0, 0, axis_index_groups=groups, tiled=True)]
where the time goes in v6:
time: 41.9 us; the launch traced here: 41.7 us
  blocking collectives  28.3 us (68%)
  waiting for transfers between devices  8.54 us (20%)
  Pallas kernels  2.88 us (7%)
  starting transfers between devices  1.29 us (3%)
  between operations  0.66 us (2%)
    all_to_all x1, blocking collectives, local(): lax.all_to_all(fields, ('date', 'az'), 0, 0, axis_index_groups=wide, tile...  17.2 us
    all_to_all x1, blocking collectives, local(): lax.all_to_all(pieces, 'date', 0, 0, axis_index_groups=groups, tiled=True)  11.1 us
    ppermute x1, waiting for transfers between devices, local(): later = lax.ppermute(own[GROUP - SPAN:], 'date', back)  8.54 us
    ppermute x1, starting transfers between devices, local(): later = lax.ppermute(own[GROUP - SPAN:], 'date', back)  1.29 us
    pallas_call x1, Pallas kernels, cut(): pl.pallas_call(cut_kernel, in_specs=[pl.BlockSpec(memory_space=pl.ANY)],...  1.26 us
  transfers between devices with their start and end apart: 1, of which 1 were waited for; matrix products, arithmetic and copies ran while one was open for 0% of the time, Pallas kernels for 1%

profile of v6, /device:TPU:1, one launch (start us, length us, event | category | flops | bytes accessed | tf_op | source)
XLA Modules:
  0.0 41.7 jit_solution(9176019578267758480)
XLA Ops:
  0.6 1.3 %cut.1 = f32[1024,128]{1,0:T(8,128)S(1)} custom-call(f32[2,32,2048]{2,1,0:T(8,128)} %bitcast.5), custom_call_target="tpu_custom_call" | custom-call | tf_op jit(solution)/shard_map/cut/pallas_call | solution.py:41
  1.9 11.1 %all_to_all.10.own_ref = f32[8,8,16,128]{3,2,1,0:T(8,128)S(1)} all-to-all(f32[8,8,16,128]{3,2,1,0:T(8,128)S(1)} %bitcast.3), channel_id=1, replica_groups={{20,28,24,16,12,8,4,0},{52,60,56,48,44,40,36,32},{84,92,88,80,76,72,68,..., dimensions={0} | all-to-all | bytes 1048576 | tf_op jit(solution)/shard_map/all_to_all | solution.py:241
  13.0 1.3 %collective-permute-start = (f32[5,8,16,128]{3,2,1,0:T(8,128)S(1)}, f32[5,8,16,128]{3,2,1,0:T(8,128)S(1)}, u32[]{:S(2)}, u32[]{:S(2)}) collective-permute-start(f32[5,8,16,128]{3,2,1,0:T(8,128)S(1)} %slice.4), channel_id=1, source_target_pairs={{32,0},{36,4},{40,8},{44,12},{48,16},{52,20},{56,24},{60,28},{64,3... | collective-permute-start | bytes 983048 | tf_op jit(solution)/shard_map/ppermute | solution.py:243
  14.3 0.5 %look_own.1.looks_ref = f32[58,128]{1,0:T(8,128)S(1)} custom-call(f32[8,8,16,128]{3,2,1,0:T(8,128)S(1)} %all_to_all.10.own_ref), custom_call_target="tpu_custom_call" | custom-call | flops 182452224 | bytes 524288 | tf_op jit(solution)/shard_map/look_own/pallas_call | solution.py:144
  14.7 8.5 %collective-permute-done.later_ref = f32[5,8,16,128]{3,2,1,0:T(8,128)S(1)} collective-permute-done((f32[5,8,16,128]{3,2,1,0:T(8,128)S(1)}, f32[5,8,16,128]{3,2,1,0:T(8,128)S(1)}, u32[]{:S(2)}, u32[]{:S(2)}) %collective-permute-start) | collective-permute-done | bytes 327712 | tf_op jit(solution)/shard_map/ppermute | solution.py:243
  23.3 0.4 look_later.1
  23.7 17.2 %all_to_all.11 = f32[32,16,128]{2,1,0:T(8,128)S(1)} all-to-all(f32[32,16,128]{2,1,0:T(8,128)S(1)} %look_later.1), channel_id=1, replica_groups={{22,20,30,28,26,24,18,16,14,12,10,8,6,4,2,0,23,21,31,29,27,25,19,17,15,..., dimensions={0} | all-to-all | bytes 524288 | tf_op jit(solution)/shard_map/all_to_all | solution.py:245
  40.9 0.8 %finish.1 = (f32[5,2,1,8,128]{4,3,2,1,0:T(8,128)}, f32[5,1,8,128]{3,2,1,0:T(8,128)}) custom-call(f32[512,128]{1,0:T(8,128)S(1)} %bitcast.4), custom_call_target="tpu_custom_call" | custom-call | tf_op jit(solution)/shard_map/finish/pallas_call | solution.py:218
  (1 shorter events, 0.0 us)
Async XLA Ops:
  13.0 10.3 %collective-permute-start = (f32[5,8,16,128]{3,2,1,0:T(8,128)S(1)}, f32[5,8,16,128]{3,2,1,0:T(8,128)S(1)}, u32[]{:S(2)}, u32[]{:S(2)}) collective-permute-start(f32[5,8,16,128]{3,2,1,0:T(8,128)S(1)} %slice.4), channel_id=1, source_target_pairs={{32,0},{36,4},{40,8},{44,12},{48,16},{52,20},{56,24},{60,28},{64,3... | collective-permute-start | bytes 983048 | tf_op jit(solution)/shard_map/ppermute | solution.py:243

commit v7 on v5

--- a/solution.py
+++ b/solution.py
@@ -13,6 +13,7 @@
 SPAN = 5
 GROUP = 8
 FIELDS = 3 * SPAN + 1
+ORDERS = ((5, 7, 6, 4, 3, 2, 1, 0), (7, 6, 5, 3, 4, 1, 0, 2))
 SUB = 16
 
 
@@ -58,6 +59,11 @@
     return (tile % 2 * GROUP + row) * (tiles // 2) + tiles // 2 - 1 - tile // 2
 
 
+def place_of(date):
+    odd = lax.rem(lax.axis_index("az"), 2) == 1
+    return jnp.where(odd, ORDERS[1].index(date), ORDERS[0].index(date))
+
+
 def look_at(date, pairs, powers, sums, cols):
     width = sums.shape[-1]
     count = 0
@@ -108,21 +114,21 @@
 
 
 def own_kernel(own_ref, out_ref, sums):
-    out_ref[...] = look_at(lambda d: planes_of(own_ref, GROUP - 1 - d), OWN_PAIRS, range(GROUP), sums, out_ref.shape[-1])
+    out_ref[...] = look_at(lambda d: planes_of(own_ref, place_of(d)), OWN_PAIRS, range(GROUP), sums, out_ref.shape[-1])
 
 
 def later_kernel(own_ref, later_ref, looks_ref, out_ref, sums, cells):
     def date(index):
         if index < GROUP:
-            return planes_of(own_ref, GROUP - 1 - index)
-        return planes_of(later_ref, GROUP + SPAN - 1 - index)
+            return planes_of(own_ref, place_of(index))
+        return planes_of(later_ref, place_of(index - GROUP) - (GROUP - SPAN))
 
     cells[...] = look_at(date, LATER_PAIRS, range(GROUP, GROUP + SPAN), sums, out_ref.shape[-1])
     tiles = out_ref.shape[0] // GROUP
     own_at = later_at = 0
     for index in range(GROUP):
         near, far = inside(index), SPAN - inside(index)
-        place = GROUP - 1 - index
+        place = ORDERS[0].index(index)
         piece = out_ref.at[at(0, place, tiles)]
         for part in range(2):
             if near:
@@ -135,7 +141,7 @@
         if far:
             piece[2 * SPAN + 1 + near :, :] = cells[LATER_ROWS : LATER_ROWS + far, :]
         for tile in range(1, tiles):
-            out_ref[at(tile, place, tiles)] = out_ref[at(0, place, tiles)]
+            out_ref[at(tile, ORDERS[tile % 2].index(index), tiles)] = out_ref[at(0, place, tiles)]
 
 
 def look_own(own, cols):
@@ -233,11 +239,13 @@
     dates, tiles = lax.axis_size("date"), lax.axis_size("az")
     _, planes, lines, samples = slabs.shape
     cols = samples // LOOK_RG
-    groups = [list(range(g, g + GROUP))[::-1] for g in range(0, dates, GROUP)]
+    both = ("date", "az")
+    starts = range(0, dates, GROUP)
+    groups = [[(g + d) * tiles + a for d in ORDERS[a % 2]] for g in starts for a in range(tiles)]
     places = sorted((at(a, row, tiles), row, a) for row in range(GROUP) for a in range(tiles))
-    wide = [[group[row] * tiles + a for _, row, a in places] for group in groups]
+    wide = [[(g + ORDERS[a % 2][row]) * tiles + a for _, row, a in places] for g in starts]
     pieces = cut(slabs[0]).reshape(GROUP, LOOK_AZ * planes, SUB, samples // SUB)
-    own = lax.all_to_all(pieces, "date", 0, 0, axis_index_groups=groups, tiled=True)
+    own = lax.all_to_all(pieces, both, 0, 0, axis_index_groups=groups, tiled=True)
     back = [(i, i - GROUP) for i in range(GROUP, dates)]
     later = lax.ppermute(own[GROUP - SPAN :], "date", back)
     fields = look_later(own, later, look_own(own, cols), tiles)

time: 42.5 us -> 42.3 us (level)
  blocking collectives: 29.2 us -> 27 us
  waiting for transfers between devices: 8.25 us -> 9.98 us
    all_to_all x1, blocking collectives: 17.1 us -> 15 us  [local(): lax.all_to_all(fields, ('date', 'az'), 0, 0, axis_index_groups=wide, tile...]
    ppermute x1, waiting for transfers between devices: 8.25 us -> 9.98 us  [local(): later = lax.ppermute(own[GROUP - SPAN:], 'date', back)]
where the time goes in v7:
time: 42.3 us; the launch traced here: 41.9 us
  blocking collectives  27 us (64%)
  waiting for transfers between devices  9.98 us (24%)
  Pallas kernels  2.89 us (7%)
  starting transfers between devices  1.29 us (3%)
  between operations  0.66 us (2%)
    all_to_all x1, blocking collectives, local(): lax.all_to_all(fields, ('date', 'az'), 0, 0, axis_index_groups=wide, tile...  15 us
    all_to_all x1, blocking collectives, local(): lax.all_to_all(pieces, both, 0, 0, axis_index_groups=groups, tiled=True)  12 us
    ppermute x1, waiting for transfers between devices, local(): later = lax.ppermute(own[GROUP - SPAN:], 'date', back)  9.98 us
    ppermute x1, starting transfers between devices, local(): later = lax.ppermute(own[GROUP - SPAN:], 'date', back)  1.29 us
    pallas_call x1, Pallas kernels, cut(): pl.pallas_call(cut_kernel, in_specs=[pl.BlockSpec(memory_space=pl.ANY)],...  1.26 us
  transfers between devices with their start and end apart: 1, of which 1 were waited for; matrix products, arithmetic and copies ran while one was open for 0% of the time, Pallas kernels for 1%

profile of v7, /device:TPU:1, one launch (start us, length us, event | category | flops | bytes accessed | tf_op | source)
XLA Modules:
  0.0 41.9 jit_solution(6389126123832130486)
XLA Ops:
  0.6 1.3 %cut.1 = f32[1024,128]{1,0:T(8,128)S(1)} custom-call(f32[2,32,2048]{2,1,0:T(8,128)} %bitcast.5), custom_call_target="tpu_custom_call" | custom-call | tf_op jit(solution)/shard_map/cut/pallas_call | solution.py:41
  1.9 12.0 %all_to_all.10.own_ref = f32[8,8,16,128]{3,2,1,0:T(8,128)S(1)} all-to-all(f32[8,8,16,128]{3,2,1,0:T(8,128)S(1)} %bitcast.3), channel_id=1, replica_groups={{20,28,24,16,12,8,4,0},{29,25,21,13,17,5,1,9},{22,30,26,18,14,10,6,2},{..., dimensions={0} | all-to-all | bytes 1048576 | tf_op jit(solution)/shard_map/all_to_all | solution.py:248
  14.0 1.3 %collective-permute-start = (f32[5,8,16,128]{3,2,1,0:T(8,128)S(1)}, f32[5,8,16,128]{3,2,1,0:T(8,128)S(1)}, u32[]{:S(2)}, u32[]{:S(2)}) collective-permute-start(f32[5,8,16,128]{3,2,1,0:T(8,128)S(1)} %slice.4), channel_id=1, source_target_pairs={{32,0},{36,4},{40,8},{44,12},{48,16},{52,20},{56,24},{60,28},{64,3... | collective-permute-start | bytes 983048 | tf_op jit(solution)/shard_map/ppermute | solution.py:250
  15.3 0.5 %look_own.1.looks_ref = f32[58,128]{1,0:T(8,128)S(1)} custom-call(f32[8,8,16,128]{3,2,1,0:T(8,128)S(1)} %all_to_all.10.own_ref), custom_call_target="tpu_custom_call" | custom-call | flops 182452224 | bytes 524288 | tf_op jit(solution)/shard_map/look_own/pallas_call | solution.py:149
  15.7 10.0 %collective-permute-done.later_ref = f32[5,8,16,128]{3,2,1,0:T(8,128)S(1)} collective-permute-done((f32[5,8,16,128]{3,2,1,0:T(8,128)S(1)}, f32[5,8,16,128]{3,2,1,0:T(8,128)S(1)}, u32[]{:S(2)}, u32[]{:S(2)}) %collective-permute-start) | collective-permute-done | bytes 327712 | tf_op jit(solution)/shard_map/ppermute | solution.py:250
  25.7 0.4 look_later.1
  26.1 15.0 %all_to_all.11 = f32[32,16,128]{2,1,0:T(8,128)S(1)} all-to-all(f32[32,16,128]{2,1,0:T(8,128)S(1)} %look_later.1), channel_id=1, replica_groups={{22,20,30,28,26,24,18,16,14,12,10,8,6,4,2,0,31,29,27,25,23,21,15,13,19,..., dimensions={0} | all-to-all | bytes 524288 | tf_op jit(solution)/shard_map/all_to_all | solution.py:252
  41.1 0.8 %finish.1 = (f32[5,2,1,8,128]{4,3,2,1,0:T(8,128)}, f32[5,1,8,128]{3,2,1,0:T(8,128)}) custom-call(f32[512,128]{1,0:T(8,128)S(1)} %bitcast.4), custom_call_target="tpu_custom_call" | custom-call | tf_op jit(solution)/shard_map/finish/pallas_call | solution.py:223
  (1 shorter events, 0.0 us)
Async XLA Ops:
  14.0 11.7 %collective-permute-start = (f32[5,8,16,128]{3,2,1,0:T(8,128)S(1)}, f32[5,8,16,128]{3,2,1,0:T(8,128)S(1)}, u32[]{:S(2)}, u32[]{:S(2)}) collective-permute-start(f32[5,8,16,128]{3,2,1,0:T(8,128)S(1)} %slice.4), channel_id=1, source_target_pairs={{32,0},{36,4},{40,8},{44,12},{48,16},{52,20},{56,24},{60,28},{64,3... | collective-permute-start | bytes 983048 | tf_op jit(solution)/shard_map/ppermute | solution.py:250

commit v8 on v6

--- a/solution.py
+++ b/solution.py
@@ -13,7 +13,7 @@
 SPAN = 5
 GROUP = 8
 FIELDS = 3 * SPAN + 1
-ORDER = (5, 7, 6, 4, 3, 2, 1, 0)
+ORDER = (6, 7, 5, 4, 2, 3, 0, 1)
 SUB = 16
 
 

time: 41.9 us -> 41.8 us (level)
  waiting for transfers between devices: 8.54 us -> 7.89 us
  blocking collectives: 28.3 us -> 28.8 us
    all_to_all x1, blocking collectives: 11.1 us -> 12.6 us  [local(): lax.all_to_all(pieces, 'date', 0, 0, axis_index_groups=groups, tiled=True)]
    all_to_all x1, blocking collectives: 17.2 us -> 16.2 us  [local(): lax.all_to_all(fields, ('date', 'az'), 0, 0, axis_index_groups=wide, tile...]
    ppermute x1, waiting for transfers between devices: 8.54 us -> 7.89 us  [local(): later = lax.ppermute(own[GROUP - SPAN:], 'date', back)]
where the time goes in v8:
time: 41.8 us; the launch traced here: 41.6 us
  blocking collectives  28.8 us (69%)
  waiting for transfers between devices  7.89 us (19%)
  Pallas kernels  2.88 us (7%)
  starting transfers between devices  1.29 us (3%)
  between operations  0.66 us (2%)
    all_to_all x1, blocking collectives, local(): lax.all_to_all(fields, ('date', 'az'), 0, 0, axis_index_groups=wide, tile...  16.2 us
    all_to_all x1, blocking collectives, local(): lax.all_to_all(pieces, 'date', 0, 0, axis_index_groups=groups, tiled=True)  12.6 us
    ppermute x1, waiting for transfers between devices, local(): later = lax.ppermute(own[GROUP - SPAN:], 'date', back)  7.89 us
    ppermute x1, starting transfers between devices, local(): later = lax.ppermute(own[GROUP - SPAN:], 'date', back)  1.29 us
    pallas_call x1, Pallas kernels, cut(): pl.pallas_call(cut_kernel, in_specs=[pl.BlockSpec(memory_space=pl.ANY)],...  1.26 us
  transfers between devices with their start and end apart: 1, of which 1 were waited for; matrix products, arithmetic and copies ran while one was open for 0% of the time, Pallas kernels for 1%

profile of v8, /device:TPU:1, one launch (start us, length us, event | category | flops | bytes accessed | tf_op | source)
XLA Modules:
  0.0 41.6 jit_solution(8481686168911240981)
XLA Ops:
  0.6 1.3 %cut.1 = f32[1024,128]{1,0:T(8,128)S(1)} custom-call(f32[2,32,2048]{2,1,0:T(8,128)} %bitcast.5), custom_call_target="tpu_custom_call" | custom-call | tf_op jit(solution)/shard_map/cut/pallas_call | solution.py:41
  1.9 12.6 %all_to_all.10.own_ref = f32[8,8,16,128]{3,2,1,0:T(8,128)S(1)} all-to-all(f32[8,8,16,128]{3,2,1,0:T(8,128)S(1)} %bitcast.3), channel_id=1, replica_groups={{24,28,20,16,8,12,0,4},{56,60,52,48,40,44,32,36},{88,92,84,80,72,76,64,..., dimensions={0} | all-to-all | bytes 1048576 | tf_op jit(solution)/shard_map/all_to_all | solution.py:241
  14.5 1.3 %collective-permute-start = (f32[5,8,16,128]{3,2,1,0:T(8,128)S(1)}, f32[5,8,16,128]{3,2,1,0:T(8,128)S(1)}, u32[]{:S(2)}, u32[]{:S(2)}) collective-permute-start(f32[5,8,16,128]{3,2,1,0:T(8,128)S(1)} %slice.4), channel_id=1, source_target_pairs={{32,0},{36,4},{40,8},{44,12},{48,16},{52,20},{56,24},{60,28},{64,3... | collective-permute-start | bytes 983048 | tf_op jit(solution)/shard_map/ppermute | solution.py:243
  15.8 0.4 %look_own.1.looks_ref = f32[58,128]{1,0:T(8,128)S(1)} custom-call(f32[8,8,16,128]{3,2,1,0:T(8,128)S(1)} %all_to_all.10.own_ref), custom_call_target="tpu_custom_call" | custom-call | flops 182452224 | bytes 524288 | tf_op jit(solution)/shard_map/look_own/pallas_call | solution.py:144
  16.3 7.9 %collective-permute-done.later_ref = f32[5,8,16,128]{3,2,1,0:T(8,128)S(1)} collective-permute-done((f32[5,8,16,128]{3,2,1,0:T(8,128)S(1)}, f32[5,8,16,128]{3,2,1,0:T(8,128)S(1)}, u32[]{:S(2)}, u32[]{:S(2)}) %collective-permute-start) | collective-permute-done | bytes 327712 | tf_op jit(solution)/shard_map/ppermute | solution.py:243
  24.2 0.4 look_later.1
  24.5 16.2 %all_to_all.11 = f32[32,16,128]{2,1,0:T(8,128)S(1)} all-to-all(f32[32,16,128]{2,1,0:T(8,128)S(1)} %look_later.1), channel_id=1, replica_groups={{26,24,30,28,22,20,18,16,10,8,14,12,2,0,6,4,27,25,31,29,23,21,19,17,11,..., dimensions={0} | all-to-all | bytes 524288 | tf_op jit(solution)/shard_map/all_to_all | solution.py:245
  40.8 0.8 %finish.1 = (f32[5,2,1,8,128]{4,3,2,1,0:T(8,128)}, f32[5,1,8,128]{3,2,1,0:T(8,128)}) custom-call(f32[512,128]{1,0:T(8,128)S(1)} %bitcast.4), custom_call_target="tpu_custom_call" | custom-call | tf_op jit(solution)/shard_map/finish/pallas_call | solution.py:218
  (1 shorter events, 0.0 us)
Async XLA Ops:
  14.5 9.6 %collective-permute-start = (f32[5,8,16,128]{3,2,1,0:T(8,128)S(1)}, f32[5,8,16,128]{3,2,1,0:T(8,128)S(1)}, u32[]{:S(2)}, u32[]{:S(2)}) collective-permute-start(f32[5,8,16,128]{3,2,1,0:T(8,128)S(1)} %slice.4), channel_id=1, source_target_pairs={{32,0},{36,4},{40,8},{44,12},{48,16},{52,20},{56,24},{60,28},{64,3... | collective-permute-start | bytes 983048 | tf_op jit(solution)/shard_map/ppermute | solution.py:243
